TPU v7x, 512 devices: a whole 4x8x8 slice. The times are simulated.
512 devices in a mesh: list: 16 (over z, core), sub: 8 (over y), slab: 4 (over x).
Axes of the slice: x: 4, y: 8, z: 8, core: 2. Of those that a mesh axis runs over, the one named last changes fastest.
Arguments:
- vectors: float32 [1024, 65536], P(None, ('list', 'sub', 'slab')), may hold values from -10 to 10
- centroids: bfloat16 [1024, 262144], P('sub', ('list', 'slab')), may hold values from -3 to 3
- codebook: float32 [32, 256, 32], P('sub'), may hold values from -10 to 10
- list_ids: int32 [65536], P(('list', 'sub', 'slab')), may hold values from 0 to 262143, as said below
Outputs:
- fresh_codebook: float32 [32, 256, 32], P('sub')
Inputs may be any that keep to these rules, and one draw needn't show every extreme that they name: `list_ids`: among the columns of one device, at most 4 name lists of one owner (list id // 4096); in every draw one owner receives exactly 4 from every device.
All inputs are finite; a program needn't handle non-finite values.
Results may differ from a plain program's by a relative error of at most 0.0003.
Values sent between devices are 32-bit elements; how exact they have to be, the bound alone decides.
A program may use at most 64 MiB of HBM per device.

v0:
```python
import math
import jax
import jax.numpy as jnp
from jax import lax
from jax.sharding import PartitionSpec as P

SOFTMAX_HEAT = 8.0
PRIOR_MASS = 1.0


def owner_rank(owner_of, owners):
    row_count = owner_of.shape[0]
    matches = (owner_of[:, None] == jnp.arange(owners)[None, :]).astype(jnp.float32)
    block = math.gcd(row_count, 128)
    blocks = matches.reshape(row_count // block, block, owners)
    strict_lower = (jnp.arange(block)[:, None] > jnp.arange(block)[None, :]).astype(jnp.float32)
    inside = jnp.einsum("ij,bjo->bio", strict_lower, blocks)
    totals = jnp.sum(blocks, axis=1)
    before = jnp.cumsum(totals, axis=0) - totals
    ranking = (inside + before[:, None, :]).reshape(row_count, owners)
    return jnp.sum(ranking * matches, axis=1).astype(jnp.int32)


def soft_sums(residual, weight, codebook):
    groups, num_codes, width = codebook.shape
    total_columns = residual.shape[1]
    block = math.gcd(total_columns, 1024)
    codeword_norm = jnp.sum(codebook * codebook, axis=-1)

    def block_step(loop_index, running):
        counts, weighted = running
        offset = (loop_index * block).astype(jnp.int32)
        column_piece = lax.dynamic_slice_in_dim(residual, offset, block, 1).reshape(
            groups, width, block
        )
        present = lax.dynamic_slice_in_dim(weight, offset, block, 0)
        inner_products = jnp.einsum(
            "skd,sdn->skn", codebook, column_piece, precision=lax.Precision.HIGHEST
        )
        assignment_scores = (2.0 * inner_products - codeword_norm[:, :, None]) / SOFTMAX_HEAT
        assignment_scores = assignment_scores - jnp.max(assignment_scores, axis=1, keepdims=True)
        exponent = jnp.exp(assignment_scores)
        assign = exponent / jnp.sum(exponent, axis=1, keepdims=True) * present[None, None, :]
        counts = counts + jnp.sum(assign, axis=2)
        weighted = weighted + jnp.einsum(
            "skn,sdn->skd", assign, column_piece, precision=lax.Precision.HIGHEST
        )
        return (counts, weighted)

    start_state = (
        jnp.zeros((groups, num_codes), jnp.float32),
        jnp.zeros((groups, num_codes, width), jnp.float32),
    )
    return lax.fori_loop(0, total_columns // block, block_step, start_state)


def refresh(counts, weighted, previous):
    return (weighted + PRIOR_MASS * previous) / (counts[:, :, None] + PRIOR_MASS)


def per_device(vectors, centroids, codebook, list_ids):
    list_count = lax.axis_size("list")
    slab_count = lax.axis_size("slab")
    sub_count = lax.axis_size("sub")
    owners = list_count * slab_count
    lists_here = centroids.shape[1]
    row_count = vectors.shape[1]
    capacity = 2 * row_count // owners
    owner_of = list_ids // lists_here
    within = (list_ids % lists_here).astype(jnp.float32)
    slot = owner_of * capacity + owner_rank(owner_of, owners)
    packed = jnp.zeros((vectors.shape[0], owners * capacity), jnp.float32).at[:, slot].set(vectors)
    labels = jnp.full((owners * capacity,), -1.0, jnp.float32).at[slot].set(within)
    labels = jnp.broadcast_to(labels[None, :], (sub_count, owners * capacity))
    arrived, arrived_labels = (
        lax.all_to_all(packed, ("list", "slab"), split_axis=1, concat_axis=1, tiled=True),
        lax.all_to_all(labels, ("list", "slab"), split_axis=1, concat_axis=1, tiled=True),
    )
    columns, column_labels = (
        lax.all_to_all(arrived, "sub", split_axis=0, concat_axis=1, tiled=True),
        lax.all_to_all(arrived_labels, "sub", split_axis=0, concat_axis=1, tiled=True),
    )
    final_labels = column_labels[0]
    present = final_labels >= 0.0
    weight = present.astype(jnp.float32)
    list_index = jnp.where(present, final_labels, 0.0).astype(jnp.int32)
    nearest = jnp.take(centroids, list_index, axis=1).astype(jnp.float32)
    residual = (columns - nearest) * weight[None, :]
    counts, weighted = soft_sums(residual, weight, codebook)
    counts, weighted = lax.psum((counts, weighted), ("list", "slab"))
    return refresh(counts, weighted, codebook)


def solution(mesh):
    return jax.shard_map(
        per_device,
        mesh=mesh,
        in_specs=(
            P(None, ("list", "sub", "slab")),
            P("sub", ("list", "slab")),
            P("sub", None, None),
            P(("list", "sub", "slab")),
        ),
        out_specs=P("sub", None, None),
        check_vma=False,
    )
```

profile of v0, /device:TPU:1, one launch (start us, length us, event | category | flops | bytes accessed | tf_op | source)
XLA Modules:
  0.0 453.4 jit_solution(12421118974912579844)
XLA Ops:
  7.5 1.0 scatter_custom_fusion.1
  9.4 14.8 %all-to-all-start.2 = ((f32[8,64,4]{0,2,1:T(4,128)}), f32[8,64,4]{0,2,1:T(4,128)S(1)}, u32[]{:S(2)}, u32[]{:S(2)}) async-start(f32[8,64,4]{0,2,1:T(4,128)} %broadcast_in_dim.61), calls=%async_computation.2 | async-start | bytes 262144 | tf_op jit(solution)/shard_map/all_to_all | solution.py:77
  24.2 1.2 copy.24
  25.5 1.3 scatter_custom_fusion
  26.8 1.3 all_to_all.34
  28.1 6.1 %all-to-all-done.2 = f32[8,64,4]{0,2,1:T(4,128)S(1)} async-done(((f32[8,64,4]{0,2,1:T(4,128)}), f32[8,64,4]{0,2,1:T(4,128)S(1)}, u32[]{:S(2)}, u32[]{:S(2)}) %all-to-all-start.2) | async-done | bytes 8224 | tf_op jit(solution)/shard_map/all_to_all | solution.py:77
  34.2 6.0 %all-to-all-start = ((f32[1024,64,4]{0,2,1:T(4,128)}), f32[1024,64,4]{0,2,1:T(4,128)S(1)}, u32[]{:S(2)}, u32[]{:S(2)}) async-start(f32[1024,64,4]{0,2,1:T(4,128)} %all_to_all.34), calls=%async_computation | async-start | bytes 2097152 | tf_op jit(solution)/shard_map/all_to_all | solution.py:76
  40.8 27.1 %all-to-all-done = f32[1024,64,4]{0,2,1:T(4,128)S(1)} async-done(((f32[1024,64,4]{0,2,1:T(4,128)}), f32[1024,64,4]{0,2,1:T(4,128)S(1)}, u32[]{:S(2)}, u32[]{:S(2)}) %all-to-all-start) | async-done | bytes 1048608 | tf_op jit(solution)/shard_map/all_to_all | solution.py:76
  68.0 6.8 %all-to-all-start.3 = ((f32[8,1,256]{2,1,0:T(1,128)}), f32[8,1,256]{2,1,0:T(1,128)S(1)}, u32[]{:S(2)}, u32[]{:S(2)}) async-start(f32[8,1,256]{2,1,0:T(1,128)} %copy.26), calls=%async_computation.3 | async-start | bytes 16384 | tf_op jit(solution)/shard_map/all_to_all | solution.py:81
  75.2 1.2 copy.25
  76.4 5.0 %all-to-all-done.3 = f32[8,1,256]{2,1,0:T(1,128)S(1)} async-done(((f32[8,1,256]{2,1,0:T(1,128)}), f32[8,1,256]{2,1,0:T(1,128)S(1)}, u32[]{:S(2)}, u32[]{:S(2)}) %all-to-all-start.3) | async-done | bytes 8224 | tf_op jit(solution)/shard_map/all_to_all | solution.py:81
  81.4 3.6 all-to-all-start.1
  85.9 6.2 %gather_fusion = bf16[2048,128]{1,0:T(8,128)(2,1)S(1)} fusion(bf16[128,4096]{0,1:T(8,128)(2,1)S(1)} %copy.27, s32[2048]{0:T(1024)S(1)} %broadcast_clamp_fusion), kind=kCustom, calls=%fused_computation | custom fusion | bytes 1056768 | tf_op jit(solution)/shard_map/jit(_take)/gather | solution.py:87
  92.1 19.6 %all-to-all-done.1 = f32[8,128,256]{1,2,0:T(8,128)S(1)} async-done(((f32[8,128,256]{1,2,0:T(8,128)}), f32[8,128,256]{1,2,0:T(8,128)S(1)}, u32[]{:S(2)}, u32[]{:S(2)}) %all-to-all-start.1) | async-done | bytes 1048608 | tf_op jit(solution)/shard_map/all_to_all | solution.py:80
  112.5 27.6 %while.16 = (s32[]{:T(128)}, f32[4,256]{1,0:T(4,128)S(1)}, f32[4,256,32]{1,2,0:T(8,128)S(1)}, f32[128,2048]{0,1:T(8,128)S(1)}, f32[4,256,32]{1,2,0:T(8,128)S(1)}...) while((s32[]{:T(128)}, f32[4,256]{1,0:T(4,128)S(1)}, ...), condition=%wide.region_9.10_spmd.clone, body=%wide.region_5.9_spmd.clone.sunk | while | flops 819004672 | bytes 41373896 | solution.py:54
  112.8 3.5 fusion.41
  116.2 3.0 fusion.42
  119.2 6.5 %fusion.44 = f32[4,256,32]{1,2,0:T(8,128)S(1)} fusion(f32[4,32,1024]{2,1,0:T(8,128)S(1)} %bitcast.61, f32[4,256,1024]{2,1,0:T(8,128)} %get-tuple-element.256, f32[1024]{0:T(1024)S(1)} %dynamic_slice.20, f32[4,1024]{1,0:T(4,128)S(1)} %get-tuple-element.257, f32[4,256,32]{1,2,0:T(8,128)S(1)} %get-tuple-element.271, pred[]{:T(512)S(6)} %compare.6), kind=kOutput, calls=%fused_computation.15.clone.1 | convolution fusion | flops 404815872 | bytes 5001217 | tf_op jit(solution)/shard_map/while/body/eval_jaxpr/skn,sdn->skd/dot_general | solution.py:45
  126.6 3.5 fusion.41
  130.0 3.0 fusion.42
  133.0 6.5 %fusion.44 = f32[4,256,32]{1,2,0:T(8,128)S(1)} fusion(f32[4,32,1024]{2,1,0:T(8,128)S(1)} %bitcast.61, f32[4,256,1024]{2,1,0:T(8,128)} %get-tuple-element.256, f32[1024]{0:T(1024)S(1)} %dynamic_slice.20, f32[4,1024]{1,0:T(4,128)S(1)} %get-tuple-element.257, f32[4,256,32]{1,2,0:T(8,128)S(1)} %get-tuple-element.271, pred[]{:T(512)S(6)} %compare.6), kind=kOutput, calls=%fused_computation.15.clone.1 | convolution fusion | flops 404815872 | bytes 5001217 | tf_op jit(solution)/shard_map/while/body/eval_jaxpr/skn,sdn->skd/dot_general | solution.py:45
  140.1 123.2 %psum.15 = f32[4,256]{1,0:T(4,128)S(1)} all-reduce(f32[4,256]{1,0:T(4,128)S(1)} %get-tuple-element.131), channel_id=1, replica_groups=mesh['list'=16,'sub'=8,'slab'=4] {'list','slab'}, use_global_device_ids=true, to_apply=%region_11.12 | all-reduce | flops 1024 | bytes 8192 | tf_op jit(solution)/shard_map/psum | solution.py:90
  263.4 181.7 %all-reduce.2.cloned.1.call-done = f32[4,256,32]{1,2,0:T(8,128)} async-done(((f32[4,256,32]{1,2,0:T(8,128)}), f32[4,256,32]{1,2,0:T(8,128)}) %all-reduce.2.cloned.1.call-update) | async-done | bytes 131088 | tf_op jit(solution)/shard_map/psum | solution.py:90
  445.0 1.6 add_divide_fusion
  (40 shorter events, 6.2 us)
Async XLA Ops:
  9.4 24.8 %all-to-all-start.2 = ((f32[8,64,4]{0,2,1:T(4,128)}), f32[8,64,4]{0,2,1:T(4,128)S(1)}, u32[]{:S(2)}, u32[]{:S(2)}) async-start(f32[8,64,4]{0,2,1:T(4,128)} %broadcast_in_dim.61), calls=%async_computation.2 | async-start | bytes 262144 | tf_op jit(solution)/shard_map/all_to_all | solution.py:77
  28.1 57.1 %copy-start.2 = (bf16[128,4096]{1,0:T(8,128)(2,1)S(1)}, bf16[128,4096]{1,0:T(8,128)(2,1)}, u32[]{:S(2)}) copy-start(bf16[128,4096]{1,0:T(8,128)(2,1)} %param.7) | copy-start | bytes 3145732
  34.2 33.8 %all-to-all-start = ((f32[1024,64,4]{0,2,1:T(4,128)}), f32[1024,64,4]{0,2,1:T(4,128)S(1)}, u32[]{:S(2)}, u32[]{:S(2)}) async-start(f32[1024,64,4]{0,2,1:T(4,128)} %all_to_all.34), calls=%async_computation | async-start | bytes 2097152 | tf_op jit(solution)/shard_map/all_to_all | solution.py:76
  68.0 13.4 %all-to-all-start.3 = ((f32[8,1,256]{2,1,0:T(1,128)}), f32[8,1,256]{2,1,0:T(1,128)S(1)}, u32[]{:S(2)}, u32[]{:S(2)}) async-start(f32[8,1,256]{2,1,0:T(1,128)} %copy.26), calls=%async_computation.3 | async-start | bytes 16384 | tf_op jit(solution)/shard_map/all_to_all | solution.py:81
  74.8 11.1 %copy-start.1 = (f32[4,256,32]{1,2,0:T(8,128)S(1)}, f32[4,256,32]{1,2,0:T(8,128)}, u32[]{:S(2)}) copy-start(f32[4,256,32]{1,2,0:T(8,128)} %param.8) | copy-start | bytes 393220
  81.4 30.4 %all-to-all-start.1 = ((f32[8,128,256]{1,2,0:T(8,128)}), f32[8,128,256]{1,2,0:T(8,128)S(1)}, u32[]{:S(2)}, u32[]{:S(2)}) async-start(f32[8,128,256]{1,2,0:T(8,128)} %copy.25), calls=%async_computation.1 | async-start | bytes 2097152 | tf_op jit(solution)/shard_map/all_to_all | solution.py:80
  84.9 360.1 %all-reduce.2.cloned.1.call-start = ((), (), s32[]{:S(2)}) async-start(), calls=%async_computation.4 | async-start | bytes 262144 | tf_op jit(solution)/shard_map/psum | solution.py:90
  119.2 6.5 %copy-start = (f32[4,256,1024]{2,1,0:T(8,128)S(1)}, f32[4,256,1024]{2,1,0:T(8,128)}, u32[]{:S(2)}) copy-start(f32[4,256,1024]{2,1,0:T(8,128)} %get-tuple-element.256) | copy-start | bytes 12582916 | tf_op jit(solution)/shard_map/while
  133.0 6.5 %copy-start = (f32[4,256,1024]{2,1,0:T(8,128)S(1)}, f32[4,256,1024]{2,1,0:T(8,128)}, u32[]{:S(2)}) copy-start(f32[4,256,1024]{2,1,0:T(8,128)} %get-tuple-element.256) | copy-start | bytes 12582916 | tf_op jit(solution)/shard_map/while
  140.1 123.2 %copy-start.3 = (f32[4,256,32]{1,2,0:T(8,128)}, f32[4,256,32]{1,2,0:T(8,128)S(1)}, u32[]{:S(2)}) copy-start(f32[4,256,32]{1,2,0:T(8,128)S(1)} %get-tuple-element.130) | copy-start | bytes 393220
Sparse Core Ops, SparseCore 0:
  263.5 181.4 all-reduce.1
where the time goes:
time: 454 us; the launch traced here: 453 us
  waiting for transfers between devices  239 us (53%)
  blocking collectives  123 us (27%)
  starting transfers between devices  31.4 us (7%)
  matrix products  20.1 us (4%)
  local copies, waits for them, and re-layouts  15.3 us (3%)
  between operations  13.6 us (3%)
  other arithmetic  10.2 us (2%)
    psum x1, waiting for transfers between devices, per_device(): counts, weighted = lax.psum((counts, weighted), ('list', 'slab'))  182 us
    psum x1, blocking collectives, per_device(): counts, weighted = lax.psum((counts, weighted), ('list', 'slab'))  123 us
    all_to_all x1, waiting for transfers between devices, per_device(): lax.all_to_all(packed, ('list', 'slab'), split_axis=1, concat_axis=1, til...  27.1 us
    all_to_all x1, waiting for transfers between devices, per_device(): lax.all_to_all(arrived, 'sub', split_axis=0, concat_axis=1, tiled=True)  19.6 us
    all_to_all x1, starting transfers between devices, per_device(): lax.all_to_all(labels, ('list', 'slab'), split_axis=1, concat_axis=1, til...  14.8 us
    dot_general x2, matrix products, block_step(): jnp.einsum('skn,sdn->skd', assign, column_piece, precision=lax.Precision....  13 us
  transfers between devices with their start and end apart: 5, of which 5 were waited for; matrix products, arithmetic and copies ran while one was open for 2% of the time, Pallas kernels for 0%

commit v1 on v0

--- a/solution.py
+++ b/solution.py
@@ -87,7 +87,9 @@
     nearest = jnp.take(centroids, list_index, axis=1).astype(jnp.float32)
     residual = (columns - nearest) * weight[None, :]
     counts, weighted = soft_sums(residual, weight, codebook)
-    counts, weighted = lax.psum((counts, weighted), ("list", "slab"))
+    counts, weighted = jax.lax.psum(
+        jax.lax.psum((counts, weighted), axis_name="slab"), axis_name="list"
+    )
     return refresh(counts, weighted, codebook)
 
 

time: 454 us -> 313 us (0.69)
  blocking collectives: 123 us -> 36.5 us
  waiting for transfers between devices: 239 us -> 185 us
    psum x1 -> x2, blocking collectives: 123 us -> 36.5 us  [the longest x1 28.2 us: per_device(): jax.lax.psum(jax.lax.psum((counts, weighted), axis_name='slab'), axis_nam...]
    psum x1 -> x2, waiting for transfers between devices: 182 us -> 127 us  [the longest x1 119 us: per_device(): jax.lax.psum(jax.lax.psum((counts, weighted), axis_name='slab'), axis_nam...]
  transfers between devices with their start and end apart: 5 -> 6, of which waited for: 5 -> 6; matrix products, arithmetic and copies ran while one was open for 2% -> 4% of each run, Pallas kernels for 0% -> 0%
where the time goes in v1:
time: 313 us; the launch traced here: 312 us
  waiting for transfers between devices  185 us (59%)
  blocking collectives  36.5 us (12%)
  starting transfers between devices  31.5 us (10%)
  matrix products  20.1 us (6%)
  local copies, waits for them, and re-layouts  15.9 us (5%)
  between operations  13.6 us (4%)
  other arithmetic  10.2 us (3%)
    psum x1, waiting for transfers between devices, per_device(): jax.lax.psum(jax.lax.psum((counts, weighted), axis_name='slab'), axis_nam...  119 us
    psum x1, blocking collectives, per_device(): jax.lax.psum(jax.lax.psum((counts, weighted), axis_name='slab'), axis_nam...  28.2 us
    all_to_all x1, waiting for transfers between devices, per_device(): lax.all_to_all(packed, ('list', 'slab'), split_axis=1, concat_axis=1, til...  27.1 us
    all_to_all x1, waiting for transfers between devices, per_device(): lax.all_to_all(arrived, 'sub', split_axis=0, concat_axis=1, tiled=True)  19.6 us
    all_to_all x1, starting transfers between devices, per_device(): lax.all_to_all(labels, ('list', 'slab'), split_axis=1, concat_axis=1, til...  14.8 us
    dot_general x2, matrix products, block_step(): jnp.einsum('skn,sdn->skd', assign, column_piece, precision=lax.Precision....  13 us
    psum x1, blocking collectives, per_device(): jax.lax.psum((counts, weighted), axis_name='slab')  8.21 us
    psum x1, waiting for transfers between devices, per_device(): jax.lax.psum((counts, weighted), axis_name='slab')  8.04 us
  transfers between devices with their start and end apart: 6, of which 6 were waited for; matrix products, arithmetic and copies ran while one was open for 4% of the time, Pallas kernels for 0%

profile of v1, /device:TPU:1, one launch (start us, length us, event | category | flops | bytes accessed | tf_op | source)
XLA Modules:
  0.0 312.5 jit_solution(11920723356979781612)
XLA Ops:
  9.4 14.8 %all-to-all-start.2 = ((f32[8,64,4]{0,2,1:T(4,128)}), f32[8,64,4]{0,2,1:T(4,128)S(1)}, u32[]{:S(2)}, u32[]{:S(2)}) async-start(f32[8,64,4]{0,2,1:T(4,128)} %broadcast_in_dim.61), calls=%async_computation.2 | async-start | bytes 262144 | tf_op jit(solution)/shard_map/all_to_all | solution.py:77
  24.2 1.2 copy.24
  25.5 1.3 scatter_custom_fusion
  26.8 1.3 all_to_all.34
  28.1 6.1 %all-to-all-done.2 = f32[8,64,4]{0,2,1:T(4,128)S(1)} async-done(((f32[8,64,4]{0,2,1:T(4,128)}), f32[8,64,4]{0,2,1:T(4,128)S(1)}, u32[]{:S(2)}, u32[]{:S(2)}) %all-to-all-start.2) | async-done | bytes 8224 | tf_op jit(solution)/shard_map/all_to_all | solution.py:77
  34.2 6.0 %all-to-all-start = ((f32[1024,64,4]{0,2,1:T(4,128)}), f32[1024,64,4]{0,2,1:T(4,128)S(1)}, u32[]{:S(2)}, u32[]{:S(2)}) async-start(f32[1024,64,4]{0,2,1:T(4,128)} %all_to_all.34), calls=%async_computation | async-start | bytes 2097152 | tf_op jit(solution)/shard_map/all_to_all | solution.py:76
  40.8 27.1 %all-to-all-done = f32[1024,64,4]{0,2,1:T(4,128)S(1)} async-done(((f32[1024,64,4]{0,2,1:T(4,128)}), f32[1024,64,4]{0,2,1:T(4,128)S(1)}, u32[]{:S(2)}, u32[]{:S(2)}) %all-to-all-start) | async-done | bytes 1048608 | tf_op jit(solution)/shard_map/all_to_all | solution.py:76
  68.0 6.8 %all-to-all-start.3 = ((f32[8,1,256]{2,1,0:T(1,128)}), f32[8,1,256]{2,1,0:T(1,128)S(1)}, u32[]{:S(2)}, u32[]{:S(2)}) async-start(f32[8,1,256]{2,1,0:T(1,128)} %copy.26), calls=%async_computation.3 | async-start | bytes 16384 | tf_op jit(solution)/shard_map/all_to_all | solution.py:81
  76.4 5.0 %all-to-all-done.3 = f32[8,1,256]{2,1,0:T(1,128)S(1)} async-done(((f32[8,1,256]{2,1,0:T(1,128)}), f32[8,1,256]{2,1,0:T(1,128)S(1)}, u32[]{:S(2)}, u32[]{:S(2)}) %all-to-all-start.3) | async-done | bytes 8224 | tf_op jit(solution)/shard_map/all_to_all | solution.py:81
  81.4 3.6 %all-to-all-start.1 = ((f32[8,128,256]{1,2,0:T(8,128)}), f32[8,128,256]{1,2,0:T(8,128)S(1)}, u32[]{:S(2)}, u32[]{:S(2)}) async-start(f32[8,128,256]{1,2,0:T(8,128)} %copy.25), calls=%async_computation.1 | async-start | bytes 2097152 | tf_op jit(solution)/shard_map/all_to_all | solution.py:80
  85.9 6.2 %gather_fusion = bf16[2048,128]{1,0:T(8,128)(2,1)S(1)} fusion(bf16[128,4096]{0,1:T(8,128)(2,1)S(1)} %copy.27, s32[2048]{0:T(1024)S(1)} %broadcast_clamp_fusion), kind=kCustom, calls=%fused_computation | custom fusion | bytes 1056768 | tf_op jit(solution)/shard_map/jit(_take)/gather | solution.py:87
  92.1 19.6 %all-to-all-done.1 = f32[8,128,256]{1,2,0:T(8,128)S(1)} async-done(((f32[8,128,256]{1,2,0:T(8,128)}), f32[8,128,256]{1,2,0:T(8,128)S(1)}, u32[]{:S(2)}, u32[]{:S(2)}) %all-to-all-start.1) | async-done | bytes 1048608 | tf_op jit(solution)/shard_map/all_to_all | solution.py:80
  112.5 27.6 %while.16 = (s32[]{:T(128)}, f32[4,256]{1,0:T(4,128)S(1)}, f32[4,256,32]{1,2,0:T(8,128)S(1)}, f32[128,2048]{0,1:T(8,128)S(1)}, f32[4,256,32]{1,2,0:T(8,128)S(1)}...) while((s32[]{:T(128)}, f32[4,256]{1,0:T(4,128)S(1)}, ...), condition=%wide.region_9.10_spmd.clone, body=%wide.region_5.9_spmd.clone.sunk | while | flops 819004672 | bytes 41373896 | solution.py:54
  112.8 3.5 %fusion.41 = f32[4,1024,256]{1,2,0:T(8,128)S(1)} fusion(f32[4,32,1024]{2,1,0:T(8,128)S(1)} %bitcast.60, f32[4,256,32]{1,2,0:T(8,128)S(1)} %get-tuple-element.284), kind=kOutput, calls=%fused_computation.56.clone.1 | convolution fusion | flops 402653184 | bytes 4849664 | tf_op jit(solution)/shard_map/while/body/eval_jaxpr/skd,sdn->skn/dot_general | solution.py:37
  116.2 3.0 fusion.42
  119.2 6.5 %fusion.44 = f32[4,256,32]{1,2,0:T(8,128)S(1)} fusion(f32[4,32,1024]{2,1,0:T(8,128)S(1)} %bitcast.61, f32[4,256,1024]{2,1,0:T(8,128)} %get-tuple-element.256, f32[1024]{0:T(1024)S(1)} %dynamic_slice.20, f32[4,1024]{1,0:T(4,128)S(1)} %get-tuple-element.257, f32[4,256,32]{1,2,0:T(8,128)S(1)} %get-tuple-element.271, pred[]{:T(512)S(6)} %compare.6), kind=kOutput, calls=%fused_computation.15.clone.1 | convolution fusion | flops 404815872 | bytes 5001217 | tf_op jit(solution)/shard_map/while/body/eval_jaxpr/skn,sdn->skd/dot_general | solution.py:45
  126.6 3.5 %fusion.41 = f32[4,1024,256]{1,2,0:T(8,128)S(1)} fusion(f32[4,32,1024]{2,1,0:T(8,128)S(1)} %bitcast.60, f32[4,256,32]{1,2,0:T(8,128)S(1)} %get-tuple-element.284), kind=kOutput, calls=%fused_computation.56.clone.1 | convolution fusion | flops 402653184 | bytes 4849664 | tf_op jit(solution)/shard_map/while/body/eval_jaxpr/skd,sdn->skn/dot_general | solution.py:37
  130.0 3.0 fusion.42
  133.0 6.5 %fusion.44 = f32[4,256,32]{1,2,0:T(8,128)S(1)} fusion(f32[4,32,1024]{2,1,0:T(8,128)S(1)} %bitcast.61, f32[4,256,1024]{2,1,0:T(8,128)} %get-tuple-element.256, f32[1024]{0:T(1024)S(1)} %dynamic_slice.20, f32[4,1024]{1,0:T(4,128)S(1)} %get-tuple-element.257, f32[4,256,32]{1,2,0:T(8,128)S(1)} %get-tuple-element.271, pred[]{:T(512)S(6)} %compare.6), kind=kOutput, calls=%fused_computation.15.clone.1 | convolution fusion | flops 404815872 | bytes 5001217 | tf_op jit(solution)/shard_map/while/body/eval_jaxpr/skn,sdn->skd/dot_general | solution.py:45
  140.8 8.2 %psum.30 = f32[4,256]{1,0:T(4,128)S(1)} all-reduce(f32[4,256]{1,0:T(4,128)S(1)} %get-tuple-element.131), channel_id=1, replica_groups=mesh['list'=16,'sub'=8,'slab'=4] {'slab'}, use_global_device_ids=true, to_apply=%region_12.13 | all-reduce | flops 1024 | bytes 8192 | tf_op jit(solution)/shard_map/psum | solution.py:91
  149.1 28.2 %psum.31 = f32[4,256]{1,0:T(4,128)S(1)} all-reduce(f32[4,256]{1,0:T(4,128)S(1)} %psum.30), channel_id=1, replica_groups=mesh['list'=16,'sub'=8,'slab'=4] {'list'}, use_global_device_ids=true, to_apply=%region_13.14 | all-reduce | flops 1024 | bytes 8192 | tf_op jit(solution)/shard_map/psum | solution.py:90
  177.3 8.0 %all-reduce.3.cloned.1.call-done = f32[4,256,32]{1,2,0:T(8,128)} async-done(((f32[4,256,32]{1,2,0:T(8,128)}), f32[4,256,32]{1,2,0:T(8,128)}) %all-reduce.3.cloned.1.call-update) | async-done | bytes 131088 | tf_op jit(solution)/shard_map/psum | solution.py:91
  185.4 118.7 %all-reduce.5.cloned.1.call-done = f32[4,256,32]{1,2,0:T(8,128)} async-done(((f32[4,256,32]{1,2,0:T(8,128)}), f32[4,256,32]{1,2,0:T(8,128)}) %all-reduce.5.cloned.1.call-update) | async-done | bytes 131088 | tf_op jit(solution)/shard_map/psum | solution.py:90
  304.0 1.6 add_divide_fusion
  (44 shorter events, 9.1 us)
Async XLA Ops:
  9.4 24.8 %all-to-all-start.2 = ((f32[8,64,4]{0,2,1:T(4,128)}), f32[8,64,4]{0,2,1:T(4,128)S(1)}, u32[]{:S(2)}, u32[]{:S(2)}) async-start(f32[8,64,4]{0,2,1:T(4,128)} %broadcast_in_dim.61), calls=%async_computation.2 | async-start | bytes 262144 | tf_op jit(solution)/shard_map/all_to_all | solution.py:77
  28.1 57.1 %copy-start.2 = (bf16[128,4096]{1,0:T(8,128)(2,1)S(1)}, bf16[128,4096]{1,0:T(8,128)(2,1)}, u32[]{:S(2)}) copy-start(bf16[128,4096]{1,0:T(8,128)(2,1)} %param.7) | copy-start | bytes 3145732
  34.2 33.8 %all-to-all-start = ((f32[1024,64,4]{0,2,1:T(4,128)}), f32[1024,64,4]{0,2,1:T(4,128)S(1)}, u32[]{:S(2)}, u32[]{:S(2)}) async-start(f32[1024,64,4]{0,2,1:T(4,128)} %all_to_all.34), calls=%async_computation | async-start | bytes 2097152 | tf_op jit(solution)/shard_map/all_to_all | solution.py:76
  68.0 13.4 %all-to-all-start.3 = ((f32[8,1,256]{2,1,0:T(1,128)}), f32[8,1,256]{2,1,0:T(1,128)S(1)}, u32[]{:S(2)}, u32[]{:S(2)}) async-start(f32[8,1,256]{2,1,0:T(1,128)} %copy.26), calls=%async_computation.3 | async-start | bytes 16384 | tf_op jit(solution)/shard_map/all_to_all | solution.py:81
  74.8 11.1 %copy-start.1 = (f32[4,256,32]{1,2,0:T(8,128)S(1)}, f32[4,256,32]{1,2,0:T(8,128)}, u32[]{:S(2)}) copy-start(f32[4,256,32]{1,2,0:T(8,128)} %param.8) | copy-start | bytes 393220
  81.4 30.4 %all-to-all-start.1 = ((f32[8,128,256]{1,2,0:T(8,128)}), f32[8,128,256]{1,2,0:T(8,128)S(1)}, u32[]{:S(2)}, u32[]{:S(2)}) async-start(f32[8,128,256]{1,2,0:T(8,128)} %copy.25), calls=%async_computation.1 | async-start | bytes 2097152 | tf_op jit(solution)/shard_map/all_to_all | solution.py:80
  84.9 100.4 %all-reduce.3.cloned.1.call-start = ((), (), s32[]{:S(2)}) async-start(), calls=%async_computation.4 | async-start | bytes 262144 | tf_op jit(solution)/shard_map/psum | solution.py:91
  119.2 6.5 %copy-start = (f32[4,256,1024]{2,1,0:T(8,128)S(1)}, f32[4,256,1024]{2,1,0:T(8,128)}, u32[]{:S(2)}) copy-start(f32[4,256,1024]{2,1,0:T(8,128)} %get-tuple-element.256) | copy-start | bytes 12582916 | tf_op jit(solution)/shard_map/while
  133.0 6.5 %copy-start = (f32[4,256,1024]{2,1,0:T(8,128)S(1)}, f32[4,256,1024]{2,1,0:T(8,128)}, u32[]{:S(2)}) copy-start(f32[4,256,1024]{2,1,0:T(8,128)} %get-tuple-element.256) | copy-start | bytes 12582916 | tf_op jit(solution)/shard_map/while
  140.1 0.7 copy-start.3
  140.8 163.3 %all-reduce.5.cloned.1.call-start = ((), (), s32[]{:S(2)}) async-start(), calls=%async_computation.5 | async-start | bytes 262144 | tf_op jit(solution)/shard_map/psum | solution.py:90
Sparse Core Ops, SparseCore 0:
  140.9 44.3 all-reduce.2
  187.8 116.2 all-reduce.4
